TPU v7x, 32 devices: a whole 2x2x4 slice. The times are simulated.
32 devices in a mesh: lat: 4 (over x, core), lon: 8 (over z, y).
Axes of the slice: x: 2, y: 2, z: 4, core: 2. Of those that a mesh axis runs over, the one named last changes fastest.
Arguments:
- state: float32 [32, 144, 192], P('lat', 'lon'), may hold values from -6 to 6
- courant_east: float32 [32, 144, 192], P('lat', 'lon'), may hold values from -0.9 to 0.9
- courant_north: float32 [32, 144, 192], P('lat', 'lon'), may hold values from -0.9 to 0.9
- cutoff: int32 [32], P('lat'), may hold values from 1 to 67, as said below
- filter_mask: int32 [32], P('lat'), may hold values from 0 to 1, as said below
Outputs:
- advanced: float32 [32, 144, 192], P('lat', 'lon')
Inputs may be any that keep to these rules, and one draw needn't show every extreme that they name: Row j's cutoff is at most 18 + 53 * d // 16, where d = min(j, 31 - j), and equals that bound on the two rows with d = 15; the two rows with d = 0 have cutoff 1. filter_mask is 0 on every row j with min(j, 31 - j) >= 8, and 1 on row 0.
All inputs are finite; a program needn't handle non-finite values.
Results may differ from a plain program's by a relative error of at most 0.00012.
Values sent between devices are 32-bit elements; how exact they have to be, the bound alone decides.
A program may use at most 64 MiB of HBM per device.

v0:
```python
import math

import jax
import jax.numpy as jnp
from jax import lax
from jax.sharding import PartitionSpec as P


def passed_along(block, axis, distance):
    devices = range(lax.axis_size(axis))
    route = [((i - distance) % len(devices), i) for i in devices]
    return lax.ppermute(block, axis, route)


def padded_2(value, sides, width):
    for axis, dim in sides:
        count, length = (lax.axis_size(axis), value.shape[dim])
        up = [(i, (i + 1) % count) for i in range(count)]
        down = [(j, i) for i, j in up]
        last = lax.slice_in_dim(value, length - width, length, axis=dim)
        initial = lax.slice_in_dim(value, 0, width, axis=dim)
        before = lax.ppermute(last, axis, up)
        after = lax.ppermute(initial, axis, down)
        value = jnp.concatenate([before, value, after], axis=dim)
    return value


def face_flux(far_lo, near_lo, near_hi, far_hi, courant):
    centred = (7.0 * (near_lo + near_hi) - (far_lo + far_hi)) / 12.0
    return courant * centred - 0.5 * jnp.abs(courant) * (near_hi - near_lo)


def build_table(n_full, n_half):
    points = jnp.arange(n_full, dtype=jnp.int32)
    waves = jnp.arange(n_half, dtype=jnp.int32)
    phase = points[:, None] * waves[None, :] % n_full
    angle = phase.astype(jnp.float32) * (2.0 * math.pi / n_full)
    return jnp.concatenate([jnp.cos(angle), jnp.sin(angle)], axis=1)


def pole_rows(field):
    return jnp.concatenate([field[:2][::-1], field[::-1][:2]], axis=0)


def send_rows(field):
    return lax.all_to_all(field, "lon", split_axis=2, concat_axis=1, tiled=True)


def return_rows(merged, lon_count):
    smooth = lax.all_to_all(merged, "lon", split_axis=1, concat_axis=2, tiled=True)
    partner = passed_along(pole_rows(smooth), "lon", lon_count // 2)
    return (smooth, partner)


def local(state, courant_east, courant_north, cutoff, filter_mask):
    n_rows, n_cols, n_comp = state.shape
    lon_count = lax.axis_size("lon")
    lat_count = lax.axis_size("lat")
    lat_index = lax.axis_index("lat")
    n_full = n_cols * lon_count
    n_half = n_full // 2 + 1
    n_lat = n_rows * lat_count
    fourier = build_table(n_full, n_half)
    waves = jnp.arange(n_half, dtype=jnp.int32)
    weights = jnp.where((waves == 0) | (waves == n_half - 1), 1.0 / n_full, 2.0 / n_full).astype(
        jnp.float32
    )
    row_lines = send_rows(state)
    kept = jnp.where(waves[None, :] <= cutoff[:, None], weights[None, :], 0.0)
    kept_both = jnp.concatenate([kept, kept], axis=1)
    coeffs = lax.dot_general(
        row_lines, fourier, (((1,), (0,)), ((), ())), precision=lax.Precision.HIGHEST
    )
    coeffs = coeffs * kept_both[:, None, :]
    synth = lax.dot_general(
        coeffs, fourier, (((2,), (1,)), ((), ())), precision=lax.Precision.HIGHEST
    )
    filtered = jnp.transpose(synth, (0, 2, 1))
    merged = jnp.where(filter_mask[:, None, None] == 1, filtered, row_lines)
    smooth, partner = return_rows(merged, lon_count)
    stacked = jnp.stack([smooth, courant_east, courant_north])
    padded = padded_2(stacked, (("lat", 1), ("lon", 2)), 2)
    zonal_p = padded[0, 2:-2]
    zonal_c = padded[1, 2:-2]
    east = face_flux(
        zonal_p[:, 0 : n_cols + 1],
        zonal_p[:, 1 : n_cols + 2],
        zonal_p[:, 2 : n_cols + 3],
        zonal_p[:, 3 : n_cols + 4],
        zonal_c[:, 1 : n_cols + 2],
    )
    zonal = -(east[:, 1:] - east[:, :-1])
    merid_p = padded[0, :, 2:-2]
    south = jnp.where(lat_index == 0, partner[:2], merid_p[:2])
    north = jnp.where(lat_index == lat_count - 1, partner[2:], merid_p[-2:])
    merid_p = jnp.concatenate([south, merid_p[2:-2], north], axis=0)
    merid_c = padded[2, :, 2:-2]
    north_flux = face_flux(
        merid_p[0 : n_rows + 1],
        merid_p[1 : n_rows + 2],
        merid_p[2 : n_rows + 3],
        merid_p[3 : n_rows + 4],
        merid_c[1 : n_rows + 2],
    )
    face_rows = lat_index * n_rows + jnp.arange(-1, n_rows, dtype=jnp.int32)
    cos_face = jnp.sin(
        jnp.minimum(face_rows + 1, n_lat - 1 - face_rows).astype(jnp.float32) * (math.pi / n_lat)
    )
    cell_rows = face_rows[1:]
    cos_cell = jnp.sin(
        (jnp.minimum(cell_rows, n_lat - 1 - cell_rows).astype(jnp.float32) + 0.5)
        * (math.pi / n_lat)
    )
    weighted = cos_face[:, None, None] * north_flux
    meridional = -(weighted[1:] - weighted[:-1]) / cos_cell[:, None, None]
    return smooth + zonal + meridional


def solution(mesh):
    placed = (
        P("lat", "lon", None),
        P("lat", "lon", None),
        P("lat", "lon", None),
        P("lat"),
        P("lat"),
    )
    return jax.shard_map(
        local, mesh=mesh, in_specs=placed, out_specs=P("lat", "lon", None), check_vma=False
    )
```

profile of v0, /device:TPU:1, one launch (start us, length us, event | category | flops | bytes accessed | tf_op | source)
XLA Modules:
  0.0 48.4 jit_solution(9552584627433358163)
XLA Ops:
  0.0 1.2 %copy.25 = f32[8,18,192]{1,0,2:T(8,128)S(1)} copy(f32[8,18,192]{2,0,1:T(8,128)} %param.5) | data formatting | bytes 221184 | tf_op args[0]
  1.2 1.3 %reshape.35 = f32[8,1,3456]{2,1,0:T(1,128)} reshape(f32[192,8,18]{2,1,0:T(8,128)S(1)} %bitcast.68) | data formatting | bytes 221184
  2.5 6.4 %all-to-all-start = ((f32[8,1,3456]{2,1,0:T(1,128)}), f32[8,1,3456]{2,1,0:T(1,128)S(1)}, u32[]{:S(2)}, u32[]{:S(2)}) async-start(f32[8,1,3456]{2,1,0:T(1,128)} %reshape.35), calls=%async_computation | async-start | bytes 221184 | tf_op jit(solution)/shard_map/all_to_all | solution.py:46
  9.3 0.6 %copy-done.2 = s32[8]{0:T(128)S(1)} copy-done((s32[8]{0:T(128)S(1)}, s32[8]{0:T(128)}, u32[]{:S(2)}) %copy-start.2) | copy-done | bytes 56
  10.1 0.6 %copy-done.3 = s32[8]{0:T(128)S(1)} copy-done((s32[8]{0:T(128)S(1)}, s32[8]{0:T(128)}, u32[]{:S(2)}) %copy-start.3) | copy-done | bytes 56
  10.7 4.4 %all-to-all-done = f32[8,1,3456]{2,1,0:T(1,128)S(1)} async-done(((f32[8,1,3456]{2,1,0:T(1,128)}), f32[8,1,3456]{2,1,0:T(1,128)S(1)}, u32[]{:S(2)}, u32[]{:S(2)}) %all-to-all-start) | async-done | bytes 110624 | tf_op jit(solution)/shard_map/all_to_all | solution.py:46
  15.1 0.5 %broadcast.87 = f32[]{:T(128)} broadcast(f32[]{:T(128)} %constant.142), dimensions={} | broadcast | bytes 8 | tf_op jit(solution)/shard_map/all_to_all | solution.py:46
  15.6 0.8 %reduce = f32[8,3456]{1,0:T(8,128)S(1)} reduce(f32[8,1,3456]{2,1,0:T(1,128)S(1)} %all-to-all-done, f32[]{:T(128)} %broadcast.87), dimensions={1}, to_apply=%all_to_all.26.reduce_sub_computation | reduce | bytes 221188 | tf_op jit(solution)/shard_map/all_to_all | solution.py:46
  16.4 0.8 %reshape.36 = f32[192,8,18]{2,1,0:T(8,128)S(1)} reshape(f32[8,3456]{1,0:T(8,128)S(1)} %reduce) | data formatting | bytes 221184
  17.2 0.5 copy.37
  18.0 0.4 fusion.20
  18.4 0.4 fusion
  19.1 1.1 %reshape.37 = f32[8,1,3456]{2,1,0:T(1,128)} reshape(f32[144,8,24]{2,1,0:T(8,128)S(1)} %bitcast.70) | data formatting | bytes 221184
  20.2 3.4 %all-to-all-start.1 = ((f32[8,1,3456]{2,1,0:T(1,128)}), f32[8,1,3456]{2,1,0:T(1,128)S(1)}, u32[]{:S(2)}, u32[]{:S(2)}) async-start(f32[8,1,3456]{2,1,0:T(1,128)} %reshape.37), calls=%async_computation.1 | async-start | bytes 221184 | tf_op jit(solution)/shard_map/all_to_all | solution.py:50
  23.6 5.9 %all-to-all-done.1 = f32[8,1,3456]{2,1,0:T(1,128)S(1)} async-done(((f32[8,1,3456]{2,1,0:T(1,128)}), f32[8,1,3456]{2,1,0:T(1,128)S(1)}, u32[]{:S(2)}, u32[]{:S(2)}) %all-to-all-start.1) | async-done | bytes 110624 | tf_op jit(solution)/shard_map/all_to_all | solution.py:50
  29.5 0.8 %reduce.1 = f32[8,3456]{1,0:T(8,128)S(1)} reduce(f32[8,1,3456]{2,1,0:T(1,128)S(1)} %all-to-all-done.1, f32[]{:T(128)} %broadcast.87), dimensions={1}, to_apply=%all_to_all.30.reduce_sub_computation | reduce | bytes 221188 | tf_op jit(solution)/shard_map/all_to_all | solution.py:50
  30.4 0.4 reshape.38
  31.4 0.7 %copy-done = f32[8,18,192]{2,0,1:T(8,128)S(1)} copy-done((f32[8,18,192]{2,0,1:T(8,128)S(1)}, f32[8,18,192]{2,0,1:T(8,128)}, u32[]{:S(2)}) %copy-start) | copy-done | bytes 110616
  32.2 4.3 %collective-permute-start = (f32[3,2,18,192]{3,1,2,0:T(2,128)S(1)}, f32[3,2,18,192]{3,1,2,0:T(2,128)S(1)}, u32[]{:S(2)}, u32[]{:S(2)}) collective-permute-start(f32[3,2,18,192]{3,1,2,0:T(2,128)S(1)} %get-tuple-element.11), channel_id=1, source_target_pairs={{0,8},{8,16},{16,24},{24,0},{1,9},{9,17},{17,25},{25,1},{2,10},{10... | collective-permute-start | bytes 248840 | tf_op jit(solution)/shard_map/ppermute | solution.py:22
  36.5 0.5 copy.33
  38.6 2.1 %collective-permute-done.1 = f32[3,2,18,192]{3,1,2,0:T(2,128)S(1)} collective-permute-done((f32[3,2,18,192]{3,1,2,0:T(2,128)S(1)}, f32[3,2,18,192]{3,1,2,0:T(2,128)S(1)}, u32[]{:S(2)}, u32[]{:S(2)}) %collective-permute-start.1) | collective-permute-done | bytes 82976 | tf_op jit(solution)/shard_map/ppermute | solution.py:23
  40.8 4.1 %collective-permute-start.3 = (f32[3,12,2,192]{3,1,2,0:T(8,128)S(1)}, f32[3,12,2,192]{3,1,2,0:T(8,128)S(1)}, u32[]{:S(2)}, u32[]{:S(2)}) collective-permute-start(f32[3,12,2,192]{3,1,2,0:T(8,128)S(1)} %get-tuple-element.10), channel_id=1, source_target_pairs={{1,0},{2,1},{3,2},{4,3},{5,4},{6,5},{7,6},{0,7},{9,8},{10,9},{11,1... | collective-permute-start | bytes 165896 | tf_op jit(solution)/shard_map/ppermute | solution.py:23
  45.3 2.3 %collective-permute-done.2 = f32[3,12,2,192]{3,1,2,0:T(8,128)S(1)} collective-permute-done((f32[3,12,2,192]{3,1,2,0:T(8,128)S(1)}, f32[3,12,2,192]{3,1,2,0:T(8,128)S(1)}, u32[]{:S(2)}, u32[]{:S(2)}) %collective-permute-start.2) | collective-permute-done | bytes 55328 | tf_op jit(solution)/shard_map/ppermute | solution.py:22
  47.7 0.8 %fusion.16 = f32[8,18,192]{2,0,1:T(8,128)} fusion(f32[9,18,192]{2,0,1:T(8,128)S(1)} %fusion.6, f32[8,18,192]{2,0,1:T(8,128)S(1)} %all_to_all.33, f32[8,19,192]{2,0,1:T(8,128)S(1)} %fusion.13, f32[8]{0:T(128)S(1)} %fusion.35), kind=kLoop, calls=%fused_computation.34 | loop fusion | flops 193536 | bytes 663584 | tf_op jit(solution)/shard_map/add | solution.py:116
  (38 shorter events, 4.0 us)
Async XLA Ops:
  2.5 12.5 %all-to-all-start = ((f32[8,1,3456]{2,1,0:T(1,128)}), f32[8,1,3456]{2,1,0:T(1,128)S(1)}, u32[]{:S(2)}, u32[]{:S(2)}) async-start(f32[8,1,3456]{2,1,0:T(1,128)} %reshape.35), calls=%async_computation | async-start | bytes 221184 | tf_op jit(solution)/shard_map/all_to_all | solution.py:46
  9.3 0.7 %copy-start.2 = (s32[8]{0:T(128)S(1)}, s32[8]{0:T(128)}, u32[]{:S(2)}) copy-start(s32[8]{0:T(128)} %param.8) | copy-start | bytes 100
  10.0 0.7 %copy-start.3 = (s32[8]{0:T(128)S(1)}, s32[8]{0:T(128)}, u32[]{:S(2)}) copy-start(s32[8]{0:T(128)} %param.9) | copy-start | bytes 100
  20.2 9.4 %all-to-all-start.1 = ((f32[8,1,3456]{2,1,0:T(1,128)}), f32[8,1,3456]{2,1,0:T(1,128)S(1)}, u32[]{:S(2)}, u32[]{:S(2)}) async-start(f32[8,1,3456]{2,1,0:T(1,128)} %reshape.37), calls=%async_computation.1 | async-start | bytes 221184 | tf_op jit(solution)/shard_map/all_to_all | solution.py:50
  31.1 0.9 %copy-start = (f32[8,18,192]{2,0,1:T(8,128)S(1)}, f32[8,18,192]{2,0,1:T(8,128)}, u32[]{:S(2)}) copy-start(f32[8,18,192]{2,0,1:T(8,128)} %param.7) | copy-start | bytes 331780
  31.2 1.0 %copy-start.1 = (f32[8,18,192]{2,0,1:T(8,128)S(1)}, f32[8,18,192]{2,0,1:T(8,128)}, u32[]{:S(2)}) copy-start(f32[8,18,192]{2,0,1:T(8,128)} %param.6) | copy-start | bytes 331780
  32.2 6.4 %collective-permute-start = (f32[3,2,18,192]{3,1,2,0:T(2,128)S(1)}, f32[3,2,18,192]{3,1,2,0:T(2,128)S(1)}, u32[]{:S(2)}, u32[]{:S(2)}) collective-permute-start(f32[3,2,18,192]{3,1,2,0:T(2,128)S(1)} %get-tuple-element.11), channel_id=1, source_target_pairs={{0,8},{8,16},{16,24},{24,0},{1,9},{9,17},{17,25},{25,1},{2,10},{10... | collective-permute-start | bytes 248840 | tf_op jit(solution)/shard_map/ppermute | solution.py:22
  36.5 4.2 %collective-permute-start.1 = (f32[3,2,18,192]{3,1,2,0:T(2,128)S(1)}, f32[3,2,18,192]{3,1,2,0:T(2,128)S(1)}, u32[]{:S(2)}, u32[]{:S(2)}) collective-permute-start(f32[3,2,18,192]{3,1,2,0:T(2,128)S(1)} %get-tuple-element.12), channel_id=1, source_target_pairs={{8,0},{16,8},{24,16},{0,24},{9,1},{17,9},{25,17},{1,25},{10,2},{18... | collective-permute-start | bytes 248840 | tf_op jit(solution)/shard_map/ppermute | solution.py:23
  38.0 6.9 %collective-permute-start.4 = (f32[4,18,192]{2,0,1:T(4,128)S(1)}, f32[4,18,192]{2,0,1:T(4,128)S(1)}, u32[]{:S(2)}, u32[]{:S(2)}) collective-permute-start(f32[4,18,192]{2,0,1:T(4,128)S(1)} %pad_maximum_fusion.22), channel_id=1, source_target_pairs={{4,0},{5,1},{6,2},{7,3},{0,4},{1,5},{2,6},{3,7},{12,8},{13,9},{14,... | collective-permute-start | bytes 165896 | tf_op jit(solution)/shard_map/ppermute | solution.py:12
  40.7 6.8 %collective-permute-start.2 = (f32[3,12,2,192]{3,1,2,0:T(8,128)S(1)}, f32[3,12,2,192]{3,1,2,0:T(8,128)S(1)}, u32[]{:S(2)}, u32[]{:S(2)}) collective-permute-start(f32[3,12,2,192]{3,1,2,0:T(8,128)S(1)} %get-tuple-element.9), channel_id=1, source_target_pairs={{0,1},{1,2},{2,3},{3,4},{4,5},{5,6},{6,7},{7,0},{8,9},{9,10},{10,1... | collective-permute-start | bytes 165896 | tf_op jit(solution)/shard_map/ppermute | solution.py:22
  40.8 6.8 %collective-permute-start.3 = (f32[3,12,2,192]{3,1,2,0:T(8,128)S(1)}, f32[3,12,2,192]{3,1,2,0:T(8,128)S(1)}, u32[]{:S(2)}, u32[]{:S(2)}) collective-permute-start(f32[3,12,2,192]{3,1,2,0:T(8,128)S(1)} %get-tuple-element.10), channel_id=1, source_target_pairs={{1,0},{2,1},{3,2},{4,3},{5,4},{6,5},{7,6},{0,7},{9,8},{10,9},{11,1... | collective-permute-start | bytes 165896 | tf_op jit(solution)/shard_map/ppermute | solution.py:23
where the time goes:
time: 49.1 us; the launch traced here: 48.4 us
  starting transfers between devices  18.5 us (38%)
  waiting for transfers between devices  15 us (31%)
  local copies, waits for them, and re-layouts  10.3 us (21%)
  other arithmetic  3.64 us (7%)
  matrix products  0.81 us (2%)
    unnamed x13, local copies, waits for them, and re-layouts  6.79 us
    all_to_all x1, starting transfers between devices, send_rows(): return lax.all_to_all(field, 'lon', split_axis=2, concat_axis=1, tiled=True)  6.38 us
    all_to_all x1, waiting for transfers between devices, return_rows(): lax.all_to_all(merged, 'lon', split_axis=1, concat_axis=2, tiled=True)  5.88 us
    all_to_all x1, waiting for transfers between devices, send_rows(): return lax.all_to_all(field, 'lon', split_axis=2, concat_axis=1, tiled=True)  4.37 us
    ppermute x2, starting transfers between devices, padded_2(): before = lax.ppermute(last, axis, up)  4.36 us
    ppermute x2, starting transfers between devices, padded_2(): after = lax.ppermute(initial, axis, down)  4.15 us
    all_to_all x1, starting transfers between devices, return_rows(): lax.all_to_all(merged, 'lon', split_axis=1, concat_axis=2, tiled=True)  3.37 us
    ppermute x2, waiting for transfers between devices, padded_2(): before = lax.ppermute(last, axis, up)  2.6 us
  transfers between devices with their start and end apart: 7, of which 5 were waited for; matrix products, arithmetic and copies ran while one was open for 5% of the time, Pallas kernels for 0%

commit v1 on v0

--- a/solution.py
+++ b/solution.py
@@ -1,9 +1,15 @@
+import functools
 import math
 
 import jax
 import jax.numpy as jnp
+import numpy as np
 from jax import lax
+from jax.experimental import pallas as pl
+from jax.experimental.pallas import tpu as pltpu
 from jax.sharding import PartitionSpec as P
+
+HIGHEST = lax.Precision.HIGHEST
 
 
 def passed_along(block, axis, distance):
@@ -116,6 +122,369 @@
     return smooth + zonal + meridional
 
 
+def spread(n_cols):
+    return -(-(n_cols + 4) // 8) * 8
+
+
+def wave_tables(n_cols, lon_count, n_lat):
+    n_full, wide = n_cols * lon_count, spread(n_cols)
+    low = n_full // 8
+    n_waves = low + (n_full // 2 - 1 - low) * (n_lat // 4 - 1) // (n_lat // 2) + 1
+    lanes = -(-2 * n_waves // 128) * 128
+    place = np.arange(wide)
+    offset = np.where(place < n_cols + 2, place, place - wide)
+    column = (np.arange(lon_count)[:, None] * n_cols + offset[None, :]).reshape(-1) % n_full
+    angle = column[:, None] * np.arange(n_waves)[None, :] % n_full * (2.0 * np.pi / n_full)
+    table = np.zeros((lon_count * wide, lanes), np.float64)
+    table[:, : 2 * n_waves] = np.concatenate([np.cos(angle), np.sin(angle)], axis=1)
+    given = np.tile((place < n_cols + 2) | (place >= wide - 2), lon_count)
+    own = np.tile(place < n_cols, lon_count)
+    synth = np.where(given[:, None], table, 0.0).astype(np.float32)
+    analyse = np.where(own[:, None], table, 0.0).T.astype(np.float32)
+    return synth, analyse, n_waves
+
+
+def fused_kernel(
+    n_waves, cut_ref, mask_ref, st_ref, ce_ref, cn_ref, t1_ref, t2_ref, out_ref,
+    blocks, lines, synth, ext, ce_wide, to_east, to_west, from_west, from_east, cn_south,
+    send_a, recv_a, send_b, recv_rows, send_c, send_raw, recv_raw, send_cn, recv_cn,
+    send_edge, recv_edge,
+):
+    n_rows, n_cols, n_comp = st_ref.shape
+    wide = blocks.shape[1]
+    n_full = n_rows * n_cols
+    lat_count, lon_count = lax.axis_size("lat"), n_rows
+    n_lat = n_rows * lat_count
+    a, i = lax.axis_index("lat"), lax.axis_index("lon")
+    southern = a < 2
+    polar = jnp.logical_or(a == 0, a == lat_count - 1)
+    other = jnp.where(southern, 1 - a, 5 - a)
+    first_edge = jnp.where(southern, n_rows - 2, 0)
+    first_pole = jnp.where(southern, 0, n_rows - 2)
+    is_edge = jnp.logical_and(i >= first_edge, i < first_edge + 2)
+    is_pole = jnp.logical_and(i >= first_pole, i < first_pole + 2)
+    east_i, west_i = lax.rem(i + 1, lon_count), lax.rem(i + lon_count - 1, lon_count)
+    half = lon_count // 2
+
+    def remote(src, dst, send, recv, lat, lon):
+        return pltpu.make_async_remote_copy(
+            src_ref=src, dst_ref=dst, send_sem=send, recv_sem=recv,
+            device_id=(lat, lon), device_id_type=pl.DeviceIdType.MESH,
+        )
+
+    barrier = pltpu.get_barrier_semaphore()
+
+    def greet(lat, lon):
+        pl.semaphore_signal(
+            barrier, inc=1, device_id=(lat, lon), device_id_type=pl.DeviceIdType.MESH
+        )
+
+    @pl.when(polar)
+    def _():
+        for step in range(1, lon_count):
+            greet(a, lax.rem(i + step, lon_count))
+
+        @pl.when(is_edge)
+        def _():
+            for lon in range(lon_count):
+                greet(other, lon)
+
+        @pl.when(jnp.logical_not(is_edge))
+        def _():
+            greet(other, i)
+
+    @pl.when(jnp.logical_not(polar))
+    def _():
+        greet(a, east_i)
+        greet(a, west_i)
+        greet(3 - a, i)
+        greet(other, first_edge)
+        greet(other, first_edge + 1)
+
+        @pl.when(jnp.logical_not(is_edge))
+        def _():
+            greet(other, i)
+
+    zero = jnp.zeros((n_rows, wide - n_cols // 8 * 8, n_comp), jnp.float32)
+    blocks[:, n_cols // 8 * 8 :, :] = zero
+    blocks[:, :n_cols, :] = st_ref[...]
+    ce_wide[:, n_cols // 8 * 8 :, :] = zero
+    ce_wide[:, :n_cols, :] = ce_ref[...]
+    to_east[2] = ce_ref[:, n_cols - 1, :]
+
+    @pl.when(jnp.logical_not(polar))
+    def _():
+        to_east[0] = st_ref[:, n_cols - 2, :]
+        to_east[1] = st_ref[:, n_cols - 1, :]
+        to_west[0] = st_ref[:, 0, :]
+        to_west[1] = st_ref[:, 1, :]
+
+    @pl.when(polar)
+    def _():
+        lines[i] = blocks[i]
+
+    @pl.when(a == 0)
+    def _():
+        cn_south[...] = jnp.zeros_like(cn_south)
+
+    @pl.when(polar)
+    def _():
+        pl.semaphore_wait(barrier, lon_count - 1 + jnp.where(is_edge, lon_count, 1))
+
+    @pl.when(jnp.logical_not(polar))
+    def _():
+        pl.semaphore_wait(barrier, 5 + jnp.where(is_edge, 0, 1))
+
+    def row_copy(step):
+        to = lax.rem(i + step, lon_count)
+        return remote(blocks.at[to], lines.at[i], send_a.at[step], recv_a.at[step], a, to)
+
+    cn_copy = remote(cn_ref.at[n_rows - 1], cn_south, send_cn, recv_cn, a + 1, i)
+    edge_ce = remote(
+        to_east.at[2], from_west.at[2], send_edge.at[0], recv_edge.at[0], a, east_i
+    )
+    edge_east = remote(to_east, from_west, send_edge.at[0], recv_edge.at[0], a, east_i)
+    edge_west = remote(to_west, from_east, send_edge.at[1], recv_edge.at[1], a, west_i)
+    raw_south = remote(
+        blocks.at[pl.ds(0, 2)], ext.at[pl.ds(n_rows + 2, 2)],
+        send_raw.at[0], recv_raw.at[1], a - 1, i,
+    )
+    raw_north = remote(
+        blocks.at[pl.ds(n_rows - 2, 2)], ext.at[pl.ds(0, 2)],
+        send_raw.at[1], recv_raw.at[0], a + 1, i,
+    )
+
+    @pl.when(polar)
+    def _():
+        for step in range(1, lon_count):
+            row_copy(step).start()
+        edge_ce.start()
+
+    @pl.when(jnp.logical_not(polar))
+    def _():
+        edge_east.start()
+        edge_west.start()
+        raw_south.start()
+        raw_north.start()
+
+    @pl.when(a < lat_count - 1)
+    def _():
+        cn_copy.start()
+
+    def line_copy(step):
+        to = lax.rem(i + step, lon_count)
+        return remote(
+            synth.at[to], ext.at[i + 2], send_b.at[step], recv_rows.at[i + 2], a, to
+        )
+
+    pole_slot = jnp.where(southern, 1 - i, n_rows * 2 + 1 - i)
+    edge_slot = jnp.where(southern, i - (n_rows - 2), n_rows + 2 + i)
+
+    def pole_copy(step):
+        to = lax.rem(i + step, lon_count)
+        return remote(
+            synth.at[lax.rem(to + half, lon_count)], ext.at[pole_slot],
+            send_c.at[step], recv_rows.at[pole_slot], a, to,
+        )
+
+    def edge_copy(lon):
+        return remote(
+            synth.at[lon], ext.at[edge_slot], send_c.at[lon], recv_rows.at[edge_slot], other, lon
+        )
+
+    def slot_wait(slot):
+        remote(blocks.at[0], ext.at[slot], send_b.at[0], recv_rows.at[slot], a, east_i).wait_recv()
+
+    @pl.when(polar)
+    def _():
+        lane = lax.broadcasted_iota(jnp.int32, (1, t1_ref.shape[1]), 1)
+        wave = jnp.where(lane < n_waves, lane, lane - n_waves)
+        kept = jnp.where(wave == 0, 1.0 / n_full, 2.0 / n_full).astype(jnp.float32)
+        kept = jnp.where(wave <= cut_ref[i], kept, 0.0)
+        weights = lax.dot_general(
+            t1_ref[...] * kept, t2_ref[...], (((1,), (0,)), ((), ())), precision=HIGHEST,
+            preferred_element_type=jnp.float32,
+        )
+        size = lon_count * wide
+        dim = (lon_count, wide, 1)
+        place = lax.broadcasted_iota(jnp.int32, dim, 1)
+        at = lax.broadcasted_iota(jnp.int32, dim, 0) * n_cols
+        at = at + jnp.where(place < n_cols + 2, place, place - wide)
+        at = jnp.where(at < 0, at + n_full, jnp.where(at >= n_full, at - n_full, at))
+        at = jnp.where((place >= n_cols + 2) & (place < wide - 2), -1, at).reshape(size, 1)
+        lane = lax.broadcasted_iota(jnp.int32, (1, size), 1)
+        start = jnp.zeros((1, size), jnp.int32)
+        for q in range(1, lon_count):
+            start = start + jnp.where(lane >= q * wide, 1, 0)
+        inner = lane - start * wide
+        source = jnp.where(inner < n_cols, start * n_cols + inner, -2)
+        weights = jnp.where(mask_ref[i] == 1, weights, jnp.where(at == source, 1.0, 0.0))
+        w_hi = weights.astype(jnp.bfloat16)
+        w_lo = (weights - w_hi.astype(jnp.float32)).astype(jnp.bfloat16)
+        for step in range(1, lon_count):
+            row_copy(step).wait_recv()
+        line = lines[...].reshape(size, n_comp)
+        l_hi = line.astype(jnp.bfloat16)
+        l_lo = (line - l_hi.astype(jnp.float32)).astype(jnp.bfloat16)
+
+        def times(left, right):
+            return lax.dot_general(
+                left, right, (((1,), (0,)), ((), ())), preferred_element_type=jnp.float32
+            )
+
+        smooth = times(w_hi, l_hi) + (times(w_hi, l_lo) + times(w_lo, l_hi))
+        synth[...] = smooth.reshape(lon_count, wide, n_comp)
+        for step in range(1, lon_count):
+            line_copy(step).start()
+
+        @pl.when(is_edge)
+        def _():
+            for lon in range(lon_count):
+                edge_copy(lon).start()
+
+        @pl.when(is_pole)
+        def _():
+            for step in range(1, lon_count):
+                pole_copy(step).start()
+            ext[pole_slot] = synth[lax.rem(i + half, lon_count)]
+
+        ext[i + 2] = synth[i]
+
+    @pl.when(jnp.logical_not(polar))
+    def _():
+        edge_east.wait_recv()
+        edge_west.wait_recv()
+        place = lax.broadcasted_iota(jnp.int32, (wide, 1), 0)
+        for r in range(n_rows):
+            row = blocks[r]
+            row = jnp.where(place == wide - 2, from_west[0, r : r + 1, :], row)
+            row = jnp.where(place == wide - 1, from_west[1, r : r + 1, :], row)
+            row = jnp.where(place == n_cols, from_east[0, r : r + 1, :], row)
+            row = jnp.where(place == n_cols + 1, from_east[1, r : r + 1, :], row)
+            ext[r + 2] = row
+
+    @pl.when(polar)
+    def _():
+        edge_ce.wait_recv()
+
+    @pl.when(a > 0)
+    def _():
+        cn_copy.wait_recv()
+
+    @pl.when(southern)
+    def _():
+        raw_south.wait_recv()
+
+    @pl.when(jnp.logical_not(southern))
+    def _():
+        raw_north.wait_recv()
+
+    @pl.when(polar)
+    def _():
+        for step in range(1, lon_count):
+            slot_wait(lax.rem(i + step, lon_count) + 2)
+        for m in range(2):
+            owner = first_pole + m
+            slot = jnp.where(southern, 1 - m, n_rows + 3 - m)
+
+            @pl.when(owner != i)
+            def _():
+                slot_wait(slot)
+
+    @pl.when(jnp.logical_not(polar))
+    def _():
+        for m in range(2):
+            slot_wait(jnp.where(southern, m, n_rows + 2 + m))
+
+    def by_lat(values):
+        chosen = jnp.float32(values[0])
+        for lat in range(1, lat_count):
+            chosen = jnp.where(a == lat, jnp.float32(values[lat]), chosen)
+        return chosen
+
+    def flux(far_lo, near_lo, near_hi, far_hi, courant):
+        centred = (7.0 * (near_lo + near_hi) - (far_lo + far_hi)) * (1.0 / 12.0)
+        return courant * centred - 0.5 * jnp.abs(courant) * (near_hi - near_lo)
+
+    place = lax.broadcasted_iota(jnp.int32, (wide, 1), 0)
+    below = None
+    for f in range(-1, n_rows):
+        faces = [lat * n_rows + f for lat in range(lat_count)]
+        cos_face = by_lat([math.sin(min(g + 1, n_lat - 1 - g) * math.pi / n_lat) for g in faces])
+        courant = cn_south[...] if f < 0 else cn_ref[f]
+        stencil = [ext[f + 1 + t, :n_cols, :] for t in range(4)]
+        weighted = cos_face * flux(*stencil, courant)
+        if f >= 0:
+            row = ext[f + 2]
+            u = jnp.where(place == wide - 1, from_west[2, f : f + 1, :], ce_wide[f])
+            east = flux(
+                pltpu.roll(row, 1, 0), row, pltpu.roll(row, wide - 1, 0),
+                pltpu.roll(row, wide - 2, 0), u,
+            )
+            zonal = -(east - pltpu.roll(east, 1, 0))
+            per_cos = by_lat(
+                [1.0 / math.sin((min(g, n_lat - 1 - g) + 0.5) * math.pi / n_lat) for g in faces]
+            )
+            out_ref[f] = (row + zonal)[:n_cols] - (weighted - below) * per_cos
+        below = weighted
+
+    @pl.when(polar)
+    def _():
+        for step in range(1, lon_count):
+            row_copy(step).wait_send()
+            line_copy(step).wait_send()
+        edge_ce.wait_send()
+
+        @pl.when(is_edge)
+        def _():
+            for lon in range(lon_count):
+                edge_copy(lon).wait_send()
+
+        @pl.when(is_pole)
+        def _():
+            for step in range(1, lon_count):
+                pole_copy(step).wait_send()
+
+    @pl.when(jnp.logical_not(polar))
+    def _():
+        edge_east.wait_send()
+        edge_west.wait_send()
+        raw_south.wait_send()
+        raw_north.wait_send()
+
+    @pl.when(a < lat_count - 1)
+    def _():
+        cn_copy.wait_send()
+
+
+def local_fused(state, courant_east, courant_north, cutoff, filter_mask):
+    n_rows, n_cols, n_comp = state.shape
+    wide = spread(n_cols)
+    synth, analyse, n_waves = wave_tables(n_cols, n_rows, n_rows * 4)
+    vmem = pl.BlockSpec(memory_space=pltpu.VMEM)
+    smem = pl.BlockSpec(memory_space=pltpu.SMEM)
+    block = pltpu.VMEM((n_rows, wide, n_comp), jnp.float32)
+    dma = pltpu.SemaphoreType.DMA
+    edge = lambda count: pltpu.VMEM((count, n_rows, n_comp), jnp.float32)
+    return pl.pallas_call(
+        functools.partial(fused_kernel, n_waves),
+        out_shape=jax.ShapeDtypeStruct(state.shape, jnp.float32),
+        in_specs=[smem, smem] + [vmem] * 5,
+        out_specs=vmem,
+        scratch_shapes=[
+            block, block, block,
+            pltpu.VMEM((n_rows + 4, wide, n_comp), jnp.float32),
+            block, edge(3), edge(2), edge(3), edge(2),
+            pltpu.VMEM((n_cols, n_comp), jnp.float32),
+            dma((n_rows,)), dma((n_rows,)), dma((n_rows,)), dma((n_rows + 4,)), dma((n_rows,)),
+            dma((2,)), dma((2,)), dma, dma, dma((2,)), dma((2,)),
+        ],
+        compiler_params=pltpu.CompilerParams(
+            collective_id=0, has_side_effects=True, vmem_limit_bytes=32 * 1024 * 1024
+        ),
+    )(cutoff, filter_mask, state, courant_east, courant_north, synth, analyse)
+
+
 def solution(mesh):
     placed = (
         P("lat", "lon", None),
@@ -124,6 +493,12 @@
         P("lat"),
         P("lat"),
     )
+
+    def dispatch(*arrays):
+        n_rows = arrays[0].shape[0]
+        row_each = mesh.shape["lat"] == 4 and mesh.shape["lon"] == n_rows and n_rows >= 8
+        return (local_fused if row_each else local)(*arrays)
+
     return jax.shard_map(
-        local, mesh=mesh, in_specs=placed, out_specs=P("lat", "lon", None), check_vma=False
-    )
+        dispatch, mesh=mesh, in_specs=placed, out_specs=P("lat", "lon", None), check_vma=False
+    )

time: 49.1 us -> 22 us (0.45)
  starting transfers between devices: 18.5 us -> 0 us
  Pallas kernels: 0 us -> 18.2 us
  waiting for transfers between devices: 15 us -> 0 us
  local copies, waits for them, and re-layouts: 10.3 us -> 3.55 us
  other arithmetic: 3.64 us -> 0 us
  matrix products: 0.81 us -> 0 us
    pallas_call x0 -> x1, Pallas kernels: none -> 18.2 us  [local_fused(): pl.pallas_call(functools.partial(fused_kernel, n_waves), out_shape=jax.Sh...]
    all_to_all x2 -> x0, waiting for transfers between devices: 10.3 us -> none  [the longest x1 5.88 us: return_rows(): lax.all_to_all(merged, 'lon', split_axis=1, concat_axis=2, tiled=True)]
    all_to_all x2 -> x0, starting transfers between devices: 9.75 us -> none  [the longest x1 6.38 us: send_rows(): return lax.all_to_all(field, 'lon', split_axis=2, concat_axis=1, tiled=True)]
    ppermute x5 -> x0, starting transfers between devices: 8.71 us -> none  [the longest x2 4.36 us: padded_2(): before = lax.ppermute(last, axis, up)]
    ppermute x5 -> x0, waiting for transfers between devices: 4.71 us -> none  [the longest x2 2.6 us: padded_2(): before = lax.ppermute(last, axis, up)]
    unnamed x13 -> x15, local copies, waits for them, and re-layouts: 6.79 us -> 2.84 us
    all_to_all x6 -> x0, local copies, waits for them, and re-layouts: 2.09 us -> none  [the longest x3 1.22 us: send_rows(): return lax.all_to_all(field, 'lon', split_axis=2, concat_axis=1, tiled=True)]
    all_to_all x2 -> x0, other arithmetic: 1.64 us -> none  [the longest x1 0.82 us: return_rows(): lax.all_to_all(merged, 'lon', split_axis=1, concat_axis=2, tiled=True)]
  transfers between devices with their start and end apart: 7 -> 0, of which waited for: 5 -> 0; matrix products, arithmetic and copies ran while one was open for 5% -> 0% of each run, Pallas kernels for 0% -> 0%
where the time goes in v1:
time: 22 us; the launch traced here: 21.8 us
  Pallas kernels  18.2 us (83%)
  local copies, waits for them, and re-layouts  3.55 us (16%)
    pallas_call x1, Pallas kernels, local_fused(): pl.pallas_call(functools.partial(fused_kernel, n_waves), out_shape=jax.Sh...  18.2 us
    unnamed x15, local copies, waits for them, and re-layouts  2.84 us
    pallas_call x1, local copies, waits for them, and re-layouts, local_fused(): pl.pallas_call(functools.partial(fused_kernel, n_waves), out_shape=jax.Sh...  0.71 us

profile of v1, /device:TPU:1, one launch (start us, length us, event | category | flops | bytes accessed | tf_op | source)
XLA Modules:
  0.0 21.8 jit_solution(15312096291691458659)
XLA Ops:
  0.0 0.0 copy-start.4
  0.0 1.0 %copy.8.st_ref = f32[8,18,192]{2,1,0:T(8,128)S(1)} copy(f32[8,18,192]{2,0,1:T(8,128)} %param.7) | data formatting | bytes 221184 | tf_op args[0]
  1.0 0.0 copy-done.4
  1.0 0.0 copy-start.5
  1.1 0.8 %copy-done.5 = f32[8,18,192]{2,0,1:T(8,128)S(1)} copy-done((f32[8,18,192]{2,0,1:T(8,128)S(1)}, f32[8,18,192]{2,0,1:T(8,128)}, u32[]{:S(2)}) %copy-start.5) | copy-done | bytes 110616
  1.9 0.0 copy-start
  1.9 0.0 copy-start.1
  1.9 0.0 copy-start.2
  1.9 0.0 copy-start.3
  2.0 0.8 %copy-done = f32[128,192]{1,0:T(8,128)S(1)} copy-done((f32[128,192]{1,0:T(8,128)S(1)}, f32[128,192]{1,0:T(8,128)}, u32[]{:S(2)}) %copy-start) | copy-done | bytes 98328
  2.8 0.1 copy-done.1
  2.9 0.0 copy-done.2
  2.9 0.0 copy-done.3
  2.9 18.2 %shard_map.73 = f32[8,18,192]{2,1,0:T(8,128)S(1)} custom-call(s32[8]{0:T(128)S(1)} %copy-done.2, s32[8]{0:T(128)S(1)} %copy-done.3, f32[8,18,192]{2,1,0:T(8,128)S(1)} %copy.8.st_ref, f32[8,18,192]{2,1,0:T(8,128)S(1)} %copy.9.ce_ref, f32[8,18,192]{2,1,0:T(8,128)S(1)} %copy.10.cn_ref, f32[192,128]{1,0:T(8,128)S(1)} %copy-done.1, f32[128,192]{1,0:T(8,128)S(1)} %copy-done), custom_call_target="tpu_custom_call" | custom-call | tf_op jit(solution)/shard_map/pallas_call | solution.py:469
  21.1 0.7 %copy.11 = f32[8,18,192]{2,0,1:T(8,128)} copy(f32[8,18,192]{2,1,0:T(8,128)S(1)} %shard_map.73) | data formatting | bytes 221184 | tf_op jit(solution)/shard_map/pallas_call | solution.py:469
  (2 shorter events, 0.1 us)
Async XLA Ops:
  0.0 1.0 %copy-start.4 = (f32[8,18,192]{2,0,1:T(8,128)S(1)}, f32[8,18,192]{2,0,1:T(8,128)}, u32[]{:S(2)}) copy-start(f32[8,18,192]{2,0,1:T(8,128)} %param.8) | copy-start | bytes 331780
  1.0 0.9 %copy-start.5 = (f32[8,18,192]{2,0,1:T(8,128)S(1)}, f32[8,18,192]{2,0,1:T(8,128)}, u32[]{:S(2)}) copy-start(f32[8,18,192]{2,0,1:T(8,128)} %param.9) | copy-start | bytes 331780
  1.9 0.9 %copy-start = (f32[128,192]{1,0:T(8,128)S(1)}, f32[128,192]{1,0:T(8,128)}, u32[]{:S(2)}) copy-start(f32[128,192]{1,0:T(8,128)} %constant.5.clone.t2_ref) | copy-start | bytes 294916
  1.9 1.0 %copy-start.1 = (f32[192,128]{1,0:T(8,128)S(1)}, f32[192,128]{1,0:T(8,128)}, u32[]{:S(2)}) copy-start(f32[192,128]{1,0:T(8,128)} %constant.4.clone.t1_ref) | copy-start | bytes 294916
  1.9 1.0 %copy-start.2 = (s32[8]{0:T(128)S(1)}, s32[8]{0:T(128)}, u32[]{:S(2)}) copy-start(s32[8]{0:T(128)} %cut_ref.1) | copy-start | bytes 100
  1.9 1.0 %copy-start.3 = (s32[8]{0:T(128)S(1)}, s32[8]{0:T(128)}, u32[]{:S(2)}) copy-start(s32[8]{0:T(128)} %mask_ref.1) | copy-start | bytes 100

commit v2 on v1

--- a/solution.py
+++ b/solution.py
@@ -145,13 +145,14 @@
 
 
 def fused_kernel(
-    n_waves, cut_ref, mask_ref, st_ref, ce_ref, cn_ref, t1_ref, t2_ref, out_ref,
-    blocks, lines, synth, ext, ce_wide, to_east, to_west, from_west, from_east, cn_south,
+    n_waves, cut_in, mask_in, st_in, ce_in, cn_in, t1_in, t2_in, out_ref,
+    cut_ref, mask_ref, st_ref, ce_ref, cn_ref, t1_ref, t2_ref, loaded,
+    blocks, lines, synth, ext, ce_rows, cn_rows, to_east, to_west, from_west, from_east, cn_south,
     send_a, recv_a, send_b, recv_rows, send_c, send_raw, recv_raw, send_cn, recv_cn,
     send_edge, recv_edge,
 ):
-    n_rows, n_cols, n_comp = st_ref.shape
-    wide = blocks.shape[1]
+    n_rows, wide, n_comp = blocks.shape
+    n_cols = st_ref.shape[0]
     n_full = n_rows * n_cols
     lat_count, lon_count = lax.axis_size("lat"), n_rows
     n_lat = n_rows * lat_count
@@ -172,6 +173,17 @@
             device_id=(lat, lon), device_id_type=pl.DeviceIdType.MESH,
         )
 
+    loads = [
+        pltpu.make_async_copy(src, dst, loaded.at[k])
+        for k, (src, dst) in enumerate(
+            [
+                (st_in, st_ref), (ce_in, ce_ref), (cn_in, cn_ref), (t1_in, t1_ref),
+                (t2_in, t2_ref), (cut_in, cut_ref), (mask_in, mask_ref),
+            ]
+        )
+    ]
+    for load in loads:
+        load.start()
     barrier = pltpu.get_barrier_semaphore()
 
     def greet(lat, lon):
@@ -205,19 +217,23 @@
         def _():
             greet(other, i)
 
-    zero = jnp.zeros((n_rows, wide - n_cols // 8 * 8, n_comp), jnp.float32)
-    blocks[:, n_cols // 8 * 8 :, :] = zero
-    blocks[:, :n_cols, :] = st_ref[...]
-    ce_wide[:, n_cols // 8 * 8 :, :] = zero
-    ce_wide[:, :n_cols, :] = ce_ref[...]
-    to_east[2] = ce_ref[:, n_cols - 1, :]
-
-    @pl.when(jnp.logical_not(polar))
-    def _():
-        to_east[0] = st_ref[:, n_cols - 2, :]
-        to_east[1] = st_ref[:, n_cols - 1, :]
-        to_west[0] = st_ref[:, 0, :]
-        to_west[1] = st_ref[:, 1, :]
+    for load in loads[:3]:
+        load.wait()
+    pad = jnp.zeros((wide - n_cols, n_rows, n_comp), jnp.float32)
+
+    def rows_first(ref):
+        return jnp.swapaxes(jnp.concatenate([ref[...], pad], axis=0), 0, 1)
+
+    blocks[...] = rows_first(st_ref)
+    cn_rows[...] = rows_first(cn_ref)
+    to_east[2] = ce_ref[n_cols - 1]
+
+    @pl.when(jnp.logical_not(polar))
+    def _():
+        to_east[0] = st_ref[n_cols - 2]
+        to_east[1] = st_ref[n_cols - 1]
+        to_west[0] = st_ref[0]
+        to_west[1] = st_ref[1]
 
     @pl.when(polar)
     def _():
@@ -239,7 +255,7 @@
         to = lax.rem(i + step, lon_count)
         return remote(blocks.at[to], lines.at[i], send_a.at[step], recv_a.at[step], a, to)
 
-    cn_copy = remote(cn_ref.at[n_rows - 1], cn_south, send_cn, recv_cn, a + 1, i)
+    cn_copy = remote(cn_rows.at[n_rows - 1], cn_south, send_cn, recv_cn, a + 1, i)
     edge_ce = remote(
         to_east.at[2], from_west.at[2], send_edge.at[0], recv_edge.at[0], a, east_i
     )
@@ -294,6 +310,10 @@
 
     def slot_wait(slot):
         remote(blocks.at[0], ext.at[slot], send_b.at[0], recv_rows.at[slot], a, east_i).wait_recv()
+
+    ce_rows[...] = rows_first(ce_ref)
+    for load in loads[3:]:
+        load.wait()
 
     @pl.when(polar)
     def _():
@@ -407,16 +427,16 @@
         return courant * centred - 0.5 * jnp.abs(courant) * (near_hi - near_lo)
 
     place = lax.broadcasted_iota(jnp.int32, (wide, 1), 0)
-    below = None
+    below, advanced = None, []
     for f in range(-1, n_rows):
         faces = [lat * n_rows + f for lat in range(lat_count)]
         cos_face = by_lat([math.sin(min(g + 1, n_lat - 1 - g) * math.pi / n_lat) for g in faces])
-        courant = cn_south[...] if f < 0 else cn_ref[f]
-        stencil = [ext[f + 1 + t, :n_cols, :] for t in range(4)]
+        courant = cn_south[...] if f < 0 else cn_rows[f]
+        stencil = [ext[f + 1 + t] for t in range(4)]
         weighted = cos_face * flux(*stencil, courant)
         if f >= 0:
             row = ext[f + 2]
-            u = jnp.where(place == wide - 1, from_west[2, f : f + 1, :], ce_wide[f])
+            u = jnp.where(place == wide - 1, from_west[2, f : f + 1, :], ce_rows[f])
             east = flux(
                 pltpu.roll(row, 1, 0), row, pltpu.roll(row, wide - 1, 0),
                 pltpu.roll(row, wide - 2, 0), u,
@@ -425,8 +445,9 @@
             per_cos = by_lat(
                 [1.0 / math.sin((min(g, n_lat - 1 - g) + 0.5) * math.pi / n_lat) for g in faces]
             )
-            out_ref[f] = (row + zonal)[:n_cols] - (weighted - below) * per_cos
+            advanced.append(row + zonal - (weighted - below) * per_cos)
         below = weighted
+    out_ref[...] = jnp.swapaxes(jnp.stack(advanced), 0, 1)[:n_cols]
 
     @pl.when(polar)
     def _():
@@ -461,28 +482,36 @@
     n_rows, n_cols, n_comp = state.shape
     wide = spread(n_cols)
     synth, analyse, n_waves = wave_tables(n_cols, n_rows, n_rows * 4)
+    flat = [
+        jnp.transpose(x, (1, 0, 2))
+        for x in (state, courant_east, courant_north)
+    ]
     vmem = pl.BlockSpec(memory_space=pltpu.VMEM)
-    smem = pl.BlockSpec(memory_space=pltpu.SMEM)
     block = pltpu.VMEM((n_rows, wide, n_comp), jnp.float32)
     dma = pltpu.SemaphoreType.DMA
+    plane = pltpu.VMEM(flat[0].shape, jnp.float32)
+    table = lambda value: pltpu.VMEM(value.shape, jnp.float32)
     edge = lambda count: pltpu.VMEM((count, n_rows, n_comp), jnp.float32)
-    return pl.pallas_call(
+    result = pl.pallas_call(
         functools.partial(fused_kernel, n_waves),
-        out_shape=jax.ShapeDtypeStruct(state.shape, jnp.float32),
-        in_specs=[smem, smem] + [vmem] * 5,
+        out_shape=jax.ShapeDtypeStruct(flat[0].shape, jnp.float32),
+        in_specs=[pl.BlockSpec(memory_space=pltpu.HBM)] * 7,
         out_specs=vmem,
         scratch_shapes=[
+            pltpu.SMEM(cutoff.shape, jnp.int32), pltpu.SMEM(cutoff.shape, jnp.int32),
+            plane, plane, plane, table(synth), table(analyse), dma((7,)),
             block, block, block,
             pltpu.VMEM((n_rows + 4, wide, n_comp), jnp.float32),
-            block, edge(3), edge(2), edge(3), edge(2),
-            pltpu.VMEM((n_cols, n_comp), jnp.float32),
+            block, block, edge(3), edge(2), edge(3), edge(2),
+            pltpu.VMEM((wide, n_comp), jnp.float32),
             dma((n_rows,)), dma((n_rows,)), dma((n_rows,)), dma((n_rows + 4,)), dma((n_rows,)),
             dma((2,)), dma((2,)), dma, dma, dma((2,)), dma((2,)),
         ],
         compiler_params=pltpu.CompilerParams(
-            collective_id=0, has_side_effects=True, vmem_limit_bytes=32 * 1024 * 1024
+            collective_id=0, has_side_effects=True
         ),
-    )(cutoff, filter_mask, state, courant_east, courant_north, synth, analyse)
+    )(cutoff, filter_mask, *flat, synth, analyse)
+    return jnp.transpose(result, (1, 0, 2))
 
 
 def solution(mesh):

time: 22 us -> 20.2 us (0.918)
  local copies, waits for them, and re-layouts: 3.55 us -> 1.58 us
    unnamed x15 -> x1, local copies, waits for them, and re-layouts: 2.84 us -> 1.58 us
    pallas_call x1 -> x0, local copies, waits for them, and re-layouts: 0.71 us -> none  [local_fused(): pl.pallas_call(functools.partial(fused_kernel, n_waves), out_shape=jax.Sh...]
where the time goes in v2:
time: 20.2 us; the launch traced here: 20 us
  Pallas kernels  18.4 us (91%)
  local copies, waits for them, and re-layouts  1.58 us (8%)
    pallas_call x1, Pallas kernels, local_fused(): pl.pallas_call(functools.partial(fused_kernel, n_waves), out_shape=jax.Sh...  18.4 us
    unnamed x1, local copies, waits for them, and re-layouts  1.58 us

profile of v2, /device:TPU:1, one launch (start us, length us, event | category | flops | bytes accessed | tf_op | source)
XLA Modules:
  0.0 20.0 jit_solution(12124314853786731972)
XLA Ops:
  0.0 18.4 %shard_map.73 = f32[18,8,192]{2,1,0:T(8,128)} custom-call(s32[8]{0:T(128)} %cut_in.1, s32[8]{0:T(128)} %mask_in.1, f32[18,8,192]{2,1,0:T(8,128)} %bitcast.5, f32[18,8,192]{2,1,0:T(8,128)} %bitcast.6, f32[18,8,192]{2,1,0:T(8,128)} %bitcast.7, f32[192,128]{1,0:T(8,128)} %constant.4.clone.t1_in, f32[128,192]{1,0:T(8,128)} %constant.5.clone.t2_in), custom_call_target="tpu_custom_call" | custom-call | tf_op jit(solution)/shard_map/pallas_call | solution.py:495
  18.4 1.6 %copy.9 = f32[8,18,192]{2,0,1:T(8,128)} copy(f32[8,18,192]{2,0,1:T(8,128)} %bitcast.4) | data formatting | bytes 221184

commit v3 on v2

--- a/solution.py
+++ b/solution.py
@@ -217,16 +217,13 @@
         def _():
             greet(other, i)
 
-    for load in loads[:3]:
-        load.wait()
+    loads[0].wait()
     pad = jnp.zeros((wide - n_cols, n_rows, n_comp), jnp.float32)
 
     def rows_first(ref):
         return jnp.swapaxes(jnp.concatenate([ref[...], pad], axis=0), 0, 1)
 
     blocks[...] = rows_first(st_ref)
-    cn_rows[...] = rows_first(cn_ref)
-    to_east[2] = ce_ref[n_cols - 1]
 
     @pl.when(jnp.logical_not(polar))
     def _():
@@ -250,6 +247,8 @@
     @pl.when(jnp.logical_not(polar))
     def _():
         pl.semaphore_wait(barrier, 5 + jnp.where(is_edge, 0, 1))
+
+    order = sorted(range(1, lon_count), key=lambda step: abs(step - half))
 
     def row_copy(step):
         to = lax.rem(i + step, lon_count)
@@ -272,16 +271,27 @@
 
     @pl.when(polar)
     def _():
-        for step in range(1, lon_count):
+        for step in order:
             row_copy(step).start()
-        edge_ce.start()
-
-    @pl.when(jnp.logical_not(polar))
-    def _():
-        edge_east.start()
+
+    @pl.when(jnp.logical_not(polar))
+    def _():
         edge_west.start()
         raw_south.start()
         raw_north.start()
+
+    for load in loads[1:3]:
+        load.wait()
+    to_east[2] = ce_ref[n_cols - 1]
+    cn_rows[...] = rows_first(cn_ref)
+
+    @pl.when(polar)
+    def _():
+        edge_ce.start()
+
+    @pl.when(jnp.logical_not(polar))
+    def _():
+        edge_east.start()
 
     @pl.when(a < lat_count - 1)
     def _():
@@ -303,9 +313,10 @@
             send_c.at[step], recv_rows.at[pole_slot], a, to,
         )
 
-    def edge_copy(lon):
+    def edge_copy(step):
+        to = lax.rem(i + step, lon_count)
         return remote(
-            synth.at[lon], ext.at[edge_slot], send_c.at[lon], recv_rows.at[edge_slot], other, lon
+            synth.at[to], ext.at[edge_slot], send_c.at[step], recv_rows.at[edge_slot], other, to
         )
 
     def slot_wait(slot):
@@ -354,19 +365,25 @@
 
         smooth = times(w_hi, l_hi) + (times(w_hi, l_lo) + times(w_lo, l_hi))
         synth[...] = smooth.reshape(lon_count, wide, n_comp)
-        for step in range(1, lon_count):
-            line_copy(step).start()
 
         @pl.when(is_edge)
         def _():
-            for lon in range(lon_count):
-                edge_copy(lon).start()
+            for step in order:
+                line_copy(step).start()
+                edge_copy(step).start()
+            edge_copy(0).start()
 
         @pl.when(is_pole)
         def _():
-            for step in range(1, lon_count):
+            for step in order:
+                line_copy(step).start()
                 pole_copy(step).start()
             ext[pole_slot] = synth[lax.rem(i + half, lon_count)]
+
+        @pl.when(jnp.logical_not(jnp.logical_or(is_edge, is_pole)))
+        def _():
+            for step in order:
+                line_copy(step).start()
 
         ext[i + 2] = synth[i]
 
@@ -427,7 +444,7 @@
         return courant * centred - 0.5 * jnp.abs(courant) * (near_hi - near_lo)
 
     place = lax.broadcasted_iota(jnp.int32, (wide, 1), 0)
-    below, advanced = None, []
+    below = None
     for f in range(-1, n_rows):
         faces = [lat * n_rows + f for lat in range(lat_count)]
         cos_face = by_lat([math.sin(min(g + 1, n_lat - 1 - g) * math.pi / n_lat) for g in faces])
@@ -445,9 +462,8 @@
             per_cos = by_lat(
                 [1.0 / math.sin((min(g, n_lat - 1 - g) + 0.5) * math.pi / n_lat) for g in faces]
             )
-            advanced.append(row + zonal - (weighted - below) * per_cos)
+            out_ref[f] = (row + zonal - (weighted - below) * per_cos)[:n_cols]
         below = weighted
-    out_ref[...] = jnp.swapaxes(jnp.stack(advanced), 0, 1)[:n_cols]
 
     @pl.when(polar)
     def _():
@@ -458,8 +474,8 @@
 
         @pl.when(is_edge)
         def _():
-            for lon in range(lon_count):
-                edge_copy(lon).wait_send()
+            for step in range(lon_count):
+                edge_copy(step).wait_send()
 
         @pl.when(is_pole)
         def _():
@@ -492,9 +508,9 @@
     plane = pltpu.VMEM(flat[0].shape, jnp.float32)
     table = lambda value: pltpu.VMEM(value.shape, jnp.float32)
     edge = lambda count: pltpu.VMEM((count, n_rows, n_comp), jnp.float32)
-    result = pl.pallas_call(
+    return pl.pallas_call(
         functools.partial(fused_kernel, n_waves),
-        out_shape=jax.ShapeDtypeStruct(flat[0].shape, jnp.float32),
+        out_shape=jax.ShapeDtypeStruct(state.shape, jnp.float32),
         in_specs=[pl.BlockSpec(memory_space=pltpu.HBM)] * 7,
         out_specs=vmem,
         scratch_shapes=[
@@ -511,7 +527,6 @@
             collective_id=0, has_side_effects=True
         ),
     )(cutoff, filter_mask, *flat, synth, analyse)
-    return jnp.transpose(result, (1, 0, 2))
 
 
 def solution(mesh):

time: 20.2 us -> 21.9 us (1.084)
  the two profiles are of different devices: /device:TPU:1 before, /device:TPU:0 now
where the time goes in v3:
time: 21.9 us; the launch traced here: 21.7 us
  Pallas kernels  20.1 us (92%)
  local copies, waits for them, and re-layouts  1.64 us (7%)
    pallas_call x1, Pallas kernels, local_fused(): pl.pallas_call(functools.partial(fused_kernel, n_waves), out_shape=jax.Sh...  20.1 us
    pallas_call x1, local copies, waits for them, and re-layouts, local_fused(): pl.pallas_call(functools.partial(fused_kernel, n_waves), out_shape=jax.Sh...  1.64 us

profile of v3, /device:TPU:0, one launch (start us, length us, event | category | flops | bytes accessed | tf_op | source)
XLA Modules:
  0.0 21.7 jit_solution(15018969713608268591)
XLA Ops:
  0.0 20.1 %shard_map.73 = f32[8,18,192]{2,1,0:T(8,128)} custom-call(s32[8]{0:T(128)} %cut_in.1, s32[8]{0:T(128)} %mask_in.1, f32[18,8,192]{2,1,0:T(8,128)} %bitcast.3, f32[18,8,192]{2,1,0:T(8,128)} %bitcast.4, f32[18,8,192]{2,1,0:T(8,128)} %bitcast.5, f32[192,128]{1,0:T(8,128)} %constant.4.clone.t1_in, f32[128,192]{1,0:T(8,128)} %constant.5.clone.t2_in), custom_call_target="tpu_custom_call" | custom-call | tf_op jit(solution)/shard_map/pallas_call | solution.py:511
  20.1 1.6 %copy.8 = f32[8,18,192]{2,0,1:T(8,128)} copy(f32[8,18,192]{2,1,0:T(8,128)} %shard_map.73) | data formatting | bytes 221184 | tf_op jit(solution)/shard_map/pallas_call | solution.py:511

commit v4 on v2

--- a/solution.py
+++ b/solution.py
@@ -217,16 +217,13 @@
         def _():
             greet(other, i)
 
-    for load in loads[:3]:
-        load.wait()
+    loads[0].wait()
     pad = jnp.zeros((wide - n_cols, n_rows, n_comp), jnp.float32)
 
     def rows_first(ref):
         return jnp.swapaxes(jnp.concatenate([ref[...], pad], axis=0), 0, 1)
 
     blocks[...] = rows_first(st_ref)
-    cn_rows[...] = rows_first(cn_ref)
-    to_east[2] = ce_ref[n_cols - 1]
 
     @pl.when(jnp.logical_not(polar))
     def _():
@@ -250,6 +247,8 @@
     @pl.when(jnp.logical_not(polar))
     def _():
         pl.semaphore_wait(barrier, 5 + jnp.where(is_edge, 0, 1))
+
+    order = sorted(range(1, lon_count), key=lambda step: -abs(step - half))
 
     def row_copy(step):
         to = lax.rem(i + step, lon_count)
@@ -272,16 +271,27 @@
 
     @pl.when(polar)
     def _():
-        for step in range(1, lon_count):
+        for step in order:
             row_copy(step).start()
-        edge_ce.start()
-
-    @pl.when(jnp.logical_not(polar))
-    def _():
-        edge_east.start()
+
+    @pl.when(jnp.logical_not(polar))
+    def _():
         edge_west.start()
         raw_south.start()
         raw_north.start()
+
+    for load in loads[1:3]:
+        load.wait()
+    to_east[2] = ce_ref[n_cols - 1]
+    cn_rows[...] = rows_first(cn_ref)
+
+    @pl.when(polar)
+    def _():
+        edge_ce.start()
+
+    @pl.when(jnp.logical_not(polar))
+    def _():
+        edge_east.start()
 
     @pl.when(a < lat_count - 1)
     def _():

time: 20.2 us -> 19 us (0.941)
  Pallas kernels: 18.4 us -> 17.3 us
    pallas_call x1, Pallas kernels: 18.4 us -> 17.3 us  [local_fused(): pl.pallas_call(functools.partial(fused_kernel, n_waves), out_shape=jax.Sh...]
where the time goes in v4:
time: 19 us; the launch traced here: 18.9 us
  Pallas kernels  17.3 us (91%)
  local copies, waits for them, and re-layouts  1.58 us (8%)
    pallas_call x1, Pallas kernels, local_fused(): pl.pallas_call(functools.partial(fused_kernel, n_waves), out_shape=jax.Sh...  17.3 us
    unnamed x1, local copies, waits for them, and re-layouts  1.58 us

profile of v4, /device:TPU:1, one launch (start us, length us, event | category | flops | bytes accessed | tf_op | source)
XLA Modules:
  0.0 18.9 jit_solution(969824289298428874)
XLA Ops:
  0.0 17.3 %shard_map.73 = f32[18,8,192]{2,1,0:T(8,128)} custom-call(s32[8]{0:T(128)} %cut_in.1, s32[8]{0:T(128)} %mask_in.1, f32[18,8,192]{2,1,0:T(8,128)} %bitcast.5, f32[18,8,192]{2,1,0:T(8,128)} %bitcast.6, f32[18,8,192]{2,1,0:T(8,128)} %bitcast.7, f32[192,128]{1,0:T(8,128)} %constant.4.clone.t1_in, f32[128,192]{1,0:T(8,128)} %constant.5.clone.t2_in), custom_call_target="tpu_custom_call" | custom-call | tf_op jit(solution)/shard_map/pallas_call | solution.py:505
  17.3 1.6 %copy.9 = f32[8,18,192]{2,0,1:T(8,128)} copy(f32[8,18,192]{2,0,1:T(8,128)} %bitcast.4) | data formatting | bytes 221184

commit v5 on v4

--- a/solution.py
+++ b/solution.py
@@ -364,7 +364,7 @@
 
         smooth = times(w_hi, l_hi) + (times(w_hi, l_lo) + times(w_lo, l_hi))
         synth[...] = smooth.reshape(lon_count, wide, n_comp)
-        for step in range(1, lon_count):
+        for step in order:
             line_copy(step).start()
 
         @pl.when(is_edge)
@@ -374,7 +374,7 @@
 
         @pl.when(is_pole)
         def _():
-            for step in range(1, lon_count):
+            for step in order:
                 pole_copy(step).start()
             ext[pole_slot] = synth[lax.rem(i + half, lon_count)]
 

time: 19 us -> 19 us (level)
  no operation moved by 1% of the time
where the time goes in v5:
time: 19 us; the launch traced here: 18.9 us
  Pallas kernels  17.3 us (91%)
  local copies, waits for them, and re-layouts  1.58 us (8%)
    pallas_call x1, Pallas kernels, local_fused(): pl.pallas_call(functools.partial(fused_kernel, n_waves), out_shape=jax.Sh...  17.3 us
    unnamed x1, local copies, waits for them, and re-layouts  1.58 us

profile of v5, /device:TPU:1, one launch (start us, length us, event | category | flops | bytes accessed | tf_op | source)
XLA Modules:
  0.0 18.9 jit_solution(3369153213149515152)
XLA Ops:
  0.0 17.3 %shard_map.73 = f32[18,8,192]{2,1,0:T(8,128)} custom-call(s32[8]{0:T(128)} %cut_in.1, s32[8]{0:T(128)} %mask_in.1, f32[18,8,192]{2,1,0:T(8,128)} %bitcast.5, f32[18,8,192]{2,1,0:T(8,128)} %bitcast.6, f32[18,8,192]{2,1,0:T(8,128)} %bitcast.7, f32[192,128]{1,0:T(8,128)} %constant.4.clone.t1_in, f32[128,192]{1,0:T(8,128)} %constant.5.clone.t2_in), custom_call_target="tpu_custom_call" | custom-call | tf_op jit(solution)/shard_map/pallas_call | solution.py:505
  17.3 1.6 %copy.9 = f32[8,18,192]{2,0,1:T(8,128)} copy(f32[8,18,192]{2,0,1:T(8,128)} %bitcast.4) | data formatting | bytes 221184
